TPU v7x, 256 devices: a whole 4x4x8 slice. The times are simulated.
256 devices in a mesh: dp: 16 (over y_lo, z), tensor: 16 (over y_hi, x, core).
Axes of the slice: x: 4, y: 4 (y_hi: 2, y_lo: 2; y = y_hi * 2 + y_lo), z: 8, core: 2. Of those that a mesh axis runs over, the one named last changes fastest.
Arguments:
- out_grad: bfloat16 [32768, 4096], P(('dp', 'tensor')), may hold values from -24 to 24
- attn_out: bfloat16 [32768, 4096], P('dp', 'tensor'), may hold values from -0.078125 to 0.078125
- o_weight: bfloat16 [4096, 4096], P('dp', 'tensor'), may hold values from -0.09375 to 0.09375
Outputs:
- attn_grad: bfloat16 [32768, 4096], P('dp', 'tensor')
- weight_grad: float32 [4096, 4096], P('dp', 'tensor')
All inputs are finite; a program needn't handle non-finite values.
Results may differ from a plain program's by a relative error of at most 0.001.
Values may be sent and summed in bfloat16 or wider, within the bound.
No kernel may reach another device: no remote copies, remote signals or barrier semaphores. Data moves between devices by JAX's collectives and lax.ppermute only.
A program may use at most 64 MiB of HBM per device.

v0:
```python
import jax
import jax.numpy as jnp
from jax import lax
from jax.sharding import PartitionSpec as P


def body(out_grad, attn_out, o_weight):
    full_weight = lax.all_gather(o_weight, "dp", axis=0, tiled=True)
    gathered = lax.all_gather(out_grad, "tensor", axis=0, tiled=True)
    attn_grad = jnp.dot(gathered, full_weight, preferred_element_type=jnp.float32).astype(
        jnp.bfloat16
    )
    weight_grad = lax.psum_scatter(
        lax.dot_general(
            gathered, attn_out, (((0,), (0,)), ((), ())), preferred_element_type=jnp.float32
        ),
        "dp",
        scatter_dimension=0,
        tiled=True,
    )
    return (attn_grad, weight_grad)


def solution(mesh):
    return jax.shard_map(
        body,
        mesh=mesh,
        in_specs=(P(("dp", "tensor"), None), P("dp", "tensor"), P("dp", "tensor")),
        out_specs=(P("dp", "tensor"), P("dp", "tensor")),
        check_vma=False,
    )
```

profile of v0, /device:TPU:2, one launch (start us, length us, event | category | flops | bytes accessed | tf_op | source)
XLA Modules:
  0.0 287.6 jit_solution(3332159857697970733)
XLA Ops:
  7.2 0.0 copy-start
  7.2 0.0 all-gather.3.cloned.1.call-start
  7.2 0.7 all-gather.3.cloned.1.call-update
  7.9 0.0 all-gather.5.cloned.1.call-start
  8.0 0.7 all-gather.5.cloned.1.call-update
  8.7 0.0 reduce-scatter.2.cloned.1.call-start
  8.7 119.1 %all-gather.3.cloned.1.call-done = bf16[2048,4096]{1,0:T(8,128)(2,1)} async-done(((bf16[128,4096]{1,0:T(8,128)(2,1)}), bf16[2048,4096]{1,0:T(8,128)(2,1)}) %all-gather.3.cloned.1.call-update) | async-done | bytes 16777232 | tf_op jit(solution)/shard_map/all_gather | solution.py:9
  127.8 0.0 copy-done
  127.8 10.2 %fusion = f32[4096,256]{1,0:T(8,128)} fusion(bf16[2048,4096]{1,0:T(8,128)(2,1)} %all-gather.3.cloned.1.call-done, bf16[2048,256]{1,0:T(8,128)(2,1)S(1)} %copy-done), kind=kOutput, calls=%fused_computation.1 | convolution fusion | flops 4294967296 | bytes 22020096 | tf_op jit(solution)/shard_map/dot_general | solution.py:14
  138.0 0.0 reduce-scatter.2.cloned.1.call-update
  138.0 62.3 %all-gather.5.cloned.1.call-done = bf16[4096,256]{1,0:T(8,128)(2,1)} async-done(((bf16[256,256]{1,0:T(8,128)(2,1)}), bf16[4096,256]{1,0:T(8,128)(2,1)}) %all-gather.5.cloned.1.call-update) | async-done | bytes 2097168 | tf_op jit(solution)/shard_map/all_gather | solution.py:8
  200.3 12.0 %convolution_convert_fusion = bf16[2048,256]{1,0:T(8,128)(2,1)} fusion(bf16[2048,4096]{1,0:T(8,128)(2,1)} %all-gather.3.cloned.1.call-done, bf16[4096,256]{1,0:T(8,128)(2,1)} %all-gather.5.cloned.1.call-done), kind=kOutput, calls=%fused_computation | convolution fusion | flops 4295491584 | bytes 19922944 | tf_op jit(solution)/shard_map/dot_general | solution.py:10
  212.3 68.8 %reduce-scatter.2.cloned.1.call-done = f32[256,256]{1,0:T(8,128)} async-done(((f32[4096,256]{1,0:T(8,128)}), f32[256,256]{1,0:T(8,128)}) %reduce-scatter.2.cloned.1.call-update) | async-done | bytes 262160 | tf_op jit(solution)/shard_map/reduce_scatter | solution.py:13
Async XLA Ops:
  7.2 120.6 %copy-start = (bf16[2048,256]{1,0:T(8,128)(2,1)S(1)}, bf16[2048,256]{1,0:T(8,128)(2,1)}, u32[]{:S(2)}) copy-start(bf16[2048,256]{1,0:T(8,128)(2,1)} %param.4) | copy-start | bytes 3145732
  7.2 120.6 %all-gather.3.cloned.1.call-start = ((), (), s32[]{:S(2)}) async-start(), calls=%async_computation.1 | async-start | bytes 17825792 | tf_op jit(solution)/shard_map/all_gather | solution.py:9
  7.9 192.4 %all-gather.5.cloned.1.call-start = ((), (), s32[]{:S(2)}) async-start(), calls=%async_computation.2 | async-start | bytes 2228224 | tf_op jit(solution)/shard_map/all_gather | solution.py:8
  8.7 272.4 %reduce-scatter.2.cloned.1.call-start = ((), (), s32[]{:S(2)}) async-start(), calls=%async_computation.3 | async-start | bytes 4456448 | tf_op jit(solution)/shard_map/reduce_scatter | solution.py:13
Sparse Core Ops, SparseCore 0:
  10.7 116.9 all-gather.2
  129.5 70.6 all-gather.4
  203.4 77.6 reduce-scatter.1
where the time goes:
time: 288 us
  waiting for transfers between devices  251 us (87%)
  matrix products  22.3 us (8%)
  between operations  13.8 us (5%)
    all_gather x1, waiting for transfers between devices, body(): gathered = lax.all_gather(out_grad, 'tensor', axis=0, tiled=True)  119 us
    reduce_scatter x1, waiting for transfers between devices, body(): lax.psum_scatter(lax.dot_general(gathered, attn_out, (((0,), (0,)), ((),...  68.8 us
    all_gather x1, waiting for transfers between devices, body(): full_weight = lax.all_gather(o_weight, 'dp', axis=0, tiled=True)  62.3 us
    dot_general x1, matrix products, body(): jnp.dot(gathered, full_weight, preferred_element_type=jnp.float32)  12 us
    dot_general x1, matrix products, body(): lax.dot_general(gathered, attn_out, (((0,), (0,)), ((), ())), preferred_e...  10.2 us
  transfers between devices with their start and end apart: 3, of which 3 were waited for; matrix products, arithmetic and copies ran while one was open for 8% of the time, Pallas kernels for 0%

commit v1 on v0

--- a/solution.py
+++ b/solution.py
@@ -5,7 +5,9 @@
 
 
 def body(out_grad, attn_out, o_weight):
-    full_weight = lax.all_gather(o_weight, "dp", axis=0, tiled=True)
+    full_weight = jnp.concatenate(
+        lax.all_to_all(jnp.stack([o_weight] * lax.axis_size("dp")), "dp", 0, 0), axis=0
+    )
     gathered = lax.all_gather(out_grad, "tensor", axis=0, tiled=True)
     attn_grad = jnp.dot(gathered, full_weight, preferred_element_type=jnp.float32).astype(
         jnp.bfloat16

time: 288 us -> 258 us (0.90)
  waiting for transfers between devices: 251 us -> 146 us
  blocking collectives: 0 us -> 76.6 us
    all_to_all x0 -> x1, blocking collectives: none -> 76.6 us  [body(): lax.all_to_all(jnp.stack([o_weight] * lax.axis_size('dp')), 'dp', 0, 0)]
    all_gather x1 -> x0, waiting for transfers between devices: 62.3 us -> none  [body(): full_weight = lax.all_gather(o_weight, 'dp', axis=0, tiled=True)]
    reduce_scatter x1, waiting for transfers between devices: 68.8 us -> 25.7 us  [body(): lax.psum_scatter(lax.dot_general(gathered, attn_out, (((0,), (0,)), ((),...]
  transfers between devices with their start and end apart: 3 -> 2, of which waited for: 3 -> 2; matrix products, arithmetic and copies ran while one was open for 8% -> 4% of each run, Pallas kernels for 0% -> 0%
where the time goes in v1:
time: 258 us
  waiting for transfers between devices  146 us (57%)
  blocking collectives  76.6 us (30%)
  matrix products  19.5 us (8%)
  between operations  14.1 us (5%)
    all_gather x1, waiting for transfers between devices, body(): gathered = lax.all_gather(out_grad, 'tensor', axis=0, tiled=True)  120 us
    all_to_all x1, blocking collectives, body(): lax.all_to_all(jnp.stack([o_weight] * lax.axis_size('dp')), 'dp', 0, 0)  76.6 us
    reduce_scatter x1, waiting for transfers between devices, body(): lax.psum_scatter(lax.dot_general(gathered, attn_out, (((0,), (0,)), ((),...  25.7 us
    dot_general x1, matrix products, body(): lax.dot_general(gathered, attn_out, (((0,), (0,)), ((), ())), preferred_e...  10.2 us
    dot_general x1, matrix products, body(): jnp.dot(gathered, full_weight, preferred_element_type=jnp.float32)  9.3 us
  transfers between devices with their start and end apart: 2, of which 2 were waited for; matrix products, arithmetic and copies ran while one was open for 4% of the time, Pallas kernels for 0%

profile of v1, /device:TPU:2, one launch (start us, length us, event | category | flops | bytes accessed | tf_op | source)
XLA Modules:
  0.0 257.5 jit_solution(2824783509480629953)
XLA Ops:
  7.2 0.0 copy-start
  7.2 0.0 all-gather.2.cloned.1.call-start
  7.2 0.7 all-gather.2.cloned.1.call-update
  7.9 0.0 reduce-scatter.2.cloned.1.call-start
  8.0 119.8 %all-gather.2.cloned.1.call-done = bf16[2048,4096]{1,0:T(8,128)(2,1)} async-done(((bf16[128,4096]{1,0:T(8,128)(2,1)}), bf16[2048,4096]{1,0:T(8,128)(2,1)}) %all-gather.2.cloned.1.call-update) | async-done | bytes 16777232 | tf_op jit(solution)/shard_map/all_gather | solution.py:11
  127.8 0.0 copy-done
  127.8 10.2 %fusion = f32[4096,256]{1,0:T(8,128)} fusion(bf16[2048,4096]{1,0:T(8,128)(2,1)} %all-gather.2.cloned.1.call-done, bf16[2048,256]{1,0:T(8,128)(2,1)S(1)} %copy-done), kind=kOutput, calls=%fused_computation.1 | convolution fusion | flops 4294967296 | bytes 22020096 | tf_op jit(solution)/shard_map/dot_general | solution.py:16
  138.0 0.0 copy-start.1
  138.0 0.0 reduce-scatter.2.cloned.1.call-update
  138.0 0.9 copy-done.1
  138.9 0.2 stack.2
  139.1 76.6 %all_to_all.5 = bf16[16,256,256]{2,1,0:T(8,128)(2,1)S(1)} all-to-all(bf16[16,256,256]{2,1,0:T(8,128)(2,1)S(1)} %stack.2), channel_id=1, replica_groups=mesh['dp'=16,'tensor'=16] {'dp'}, dimensions={0} | all-to-all | bytes 4194304 | tf_op jit(solution)/shard_map/all_to_all | solution.py:9
  215.6 9.3 %convolution_convert_fusion = bf16[2048,256]{1,0:T(8,128)(2,1)} fusion(bf16[2048,4096]{1,0:T(8,128)(2,1)} %all-gather.2.cloned.1.call-done, bf16[4096,256]{1,0:T(8,128)(2,1)S(1)} %bitcast.5), kind=kOutput, calls=%fused_computation | convolution fusion | flops 4295491584 | bytes 19922944 | tf_op jit(solution)/shard_map/dot_general | solution.py:12
  225.0 25.7 %reduce-scatter.2.cloned.1.call-done = f32[256,256]{1,0:T(8,128)} async-done(((f32[4096,256]{1,0:T(8,128)}), f32[256,256]{1,0:T(8,128)}) %reduce-scatter.2.cloned.1.call-update) | async-done | bytes 262160 | tf_op jit(solution)/shard_map/reduce_scatter | solution.py:15
Async XLA Ops:
  7.2 120.6 %copy-start = (bf16[2048,256]{1,0:T(8,128)(2,1)S(1)}, bf16[2048,256]{1,0:T(8,128)(2,1)}, u32[]{:S(2)}) copy-start(bf16[2048,256]{1,0:T(8,128)(2,1)} %param.4) | copy-start | bytes 3145732
  7.2 120.6 %all-gather.2.cloned.1.call-start = ((), (), s32[]{:S(2)}) async-start(), calls=%async_computation.2 | async-start | bytes 17825792 | tf_op jit(solution)/shard_map/all_gather | solution.py:11
  7.9 242.7 %reduce-scatter.2.cloned.1.call-start = ((), (), s32[]{:S(2)}) async-start(), calls=%async_computation.3 | async-start | bytes 4456448 | tf_op jit(solution)/shard_map/reduce_scatter | solution.py:15
  138.0 0.9 copy-start.1
Sparse Core Ops, SparseCore 0:
  10.7 116.9 all-gather.1
  138.1 112.4 reduce-scatter.1
